TPU v7x, 32 devices: a whole 2x2x4 slice. The times are simulated.
32 devices in a mesh: groups: 2 (over y), seq: 4 (over z), head: 2 (over x), sub: 2 (over core).
Axes of the slice: x: 2, y: 2, z: 4, core: 2. Of those that a mesh axis runs over, the one named last changes fastest.
Arguments:
- queries: bfloat16 [8192, 2048], P(('groups', 'seq', 'sub'), 'head'), parts along dimension 0, may hold values from -4.5 to 4.5
- keys: bfloat16 [8192, 2048], P(('groups', 'seq', 'sub'), 'head'), parts along dimension 0, may hold values from -4.5 to 4.5
- values: bfloat16 [8192, 2048], P(('groups', 'seq', 'sub'), 'head'), parts along dimension 0, may hold values from -6 to 6
- grad_out: bfloat16 [8192, 2048], P(('groups', 'seq', 'sub'), 'head'), parts along dimension 0, may hold values from -6 to 6
- cluster_ids: int32 [16, 8192, 1], P('head', ('groups', 'seq', 'sub')), parts along dimension 1, may hold values from 0 to 63; in each aligned block of 512 rows (0 to 511, 512 to 1023, ..., all dimensions but the last counted through in order) at most 12 rows name the same one
Outputs:
- attention: bfloat16 [8192, 2048], P(('groups', 'seq', 'sub'), 'head'), parts along dimension 0
- grad_queries: bfloat16 [8192, 2048], P(('groups', 'seq', 'sub'), 'head'), parts along dimension 0
- grad_keys: bfloat16 [8192, 2048], P(('groups', 'seq', 'sub'), 'head'), parts along dimension 0
- grad_values: bfloat16 [8192, 2048], P(('groups', 'seq', 'sub'), 'head'), parts along dimension 0
- centroid_sums: float32 [16, 128, 128], P('head', 'groups'), parts along dimension 1
There are 2 independent parts, one for each index of `groups`. A program takes and returns all parts, laid end to end along the dimension named above; each array names one. Nothing has to cross between parts.
Inputs may be any that keep to these rules, and one draw needn't show every extreme that they name: `cluster_ids`: in each head, the tokens of one device (aligned blocks of 512 tokens) name one cluster at most 12 times, a bound that some block reaches.
All inputs are finite; a program needn't handle non-finite values.
Results may differ from a plain program's by a relative error of at most 0.0052.
Values may be sent and summed in bfloat16 or wider, within the bound.
A program may use at most 128 MiB of HBM per device.

v0:
```python
import functools
import jax
import jax.numpy as jnp
from jax import lax
from jax.experimental import pallas as pl
from jax.experimental.pallas import tpu as pltpu
from jax.sharding import PartitionSpec as P

CLUSTERS = 64
CAP = 12
SLOT = 16
AXES = ("seq", "sub")
VMEM = 56 * 1024 * 1024


norm_eps = 1e-06
masked_score = -1e30


def unit_rows(matrix):
    return matrix * lax.rsqrt(jnp.sum(matrix * matrix, axis=-1, keepdims=True) + norm_eps)


def cluster_work(packed, counts):
    head_width = packed.shape[-1] // 4
    row_count = packed.shape[2]
    slot_rank = (jnp.arange(row_count) % CAP).astype(jnp.float32)
    filled = jnp.repeat(counts.astype(jnp.float32), CAP, axis=2)
    filled_slot = slot_rank[None, None, :] < filled
    query_rows = packed[..., :head_width]
    key_rows = packed[..., head_width : 2 * head_width]
    value_rows = packed[..., 2 * head_width : 3 * head_width]
    grad_rows = packed[..., 3 * head_width :]
    score_scale = head_width ** (-0.5)
    scores = (
        jnp.einsum("hcqd,hckd->hcqk", query_rows, key_rows, preferred_element_type=jnp.float32)
        * score_scale
    )
    scores = jnp.where(filled_slot[:, :, None, :], scores, masked_score)
    row_max = jnp.max(scores, axis=-1, keepdims=True)
    exp_scores = jnp.exp(scores - row_max)
    probabilities = exp_scores / jnp.sum(exp_scores, axis=-1, keepdims=True)
    weights = probabilities.astype(jnp.bfloat16)
    attention = jnp.einsum(
        "hcqk,hckd->hcqd", weights, value_rows, preferred_element_type=jnp.float32
    ).astype(jnp.bfloat16)
    dprobs = jnp.einsum(
        "hcqd,hckd->hcqk", grad_rows, value_rows, preferred_element_type=jnp.float32
    )
    row_delta = jnp.sum(probabilities * dprobs, axis=-1, keepdims=True)
    dscore = (score_scale * probabilities * (dprobs - row_delta)).astype(jnp.bfloat16)
    dquery = jnp.einsum(
        "hcqk,hckd->hcqd", dscore, key_rows, preferred_element_type=jnp.float32
    ).astype(jnp.bfloat16)
    dkey = jnp.einsum(
        "hcqk,hcqd->hckd", dscore, query_rows, preferred_element_type=jnp.float32
    ).astype(jnp.bfloat16)
    dvalue = jnp.einsum(
        "hcqk,hcqd->hckd", weights, grad_rows, preferred_element_type=jnp.float32
    ).astype(jnp.bfloat16)
    result = jnp.concatenate([attention, dquery, dkey, dvalue], axis=-1)
    cluster_sums = None
    return (result, cluster_sums)


def padded_path(queries, keys, values, grad_out, cluster_ids):
    tok_rows = queries.shape[0]
    heads_here = cluster_ids.shape[0]
    head_width = queries.shape[1] // heads_here
    cluster_of = cluster_ids[:, :, 0]
    member = (
        cluster_of[:, :, None] == jnp.arange(CLUSTERS, dtype=jnp.int32)[None, None, :]
    ).astype(jnp.int32)
    before = jnp.cumsum(member, axis=1) - member
    slot_rank = jnp.sum(before * member, axis=2)
    slot_index = cluster_of * CAP + slot_rank
    dispatch = (
        slot_index[:, None, :] == jnp.arange(CLUSTERS * CAP, dtype=jnp.int32)[None, :, None]
    ).astype(jnp.bfloat16)
    counts = jnp.sum(member, axis=1).astype(jnp.bfloat16)[:, :, None]
    head_shape = (tok_rows, heads_here, head_width)
    stacked = jnp.stack(
        [
            queries.reshape(head_shape),
            keys.reshape(head_shape),
            values.reshape(head_shape),
            grad_out.reshape(head_shape),
        ],
        axis=2,
    )
    packed = jnp.einsum(
        "hst,thfd->hsfd", dispatch, stacked, preferred_element_type=jnp.float32
    ).astype(jnp.bfloat16)
    packed = packed.reshape(heads_here, CLUSTERS, CAP, 4 * head_width)
    result, _ = cluster_work(
        lax.all_to_all(packed, AXES, split_axis=1, concat_axis=2, tiled=True),
        lax.all_to_all(counts, AXES, split_axis=1, concat_axis=2, tiled=True),
    )
    sent_back = lax.all_to_all(result, AXES, split_axis=2, concat_axis=1, tiled=True)
    rows_back = sent_back.reshape(heads_here, CLUSTERS * CAP, 4, head_width)
    merged = jnp.einsum(
        "hst,hsfd->thfd", dispatch, rows_back, preferred_element_type=jnp.float32
    ).astype(jnp.bfloat16)
    flat_shape = (tok_rows, heads_here * head_width)
    return tuple(merged[:, :, i, :].reshape(flat_shape) for i in range(4))


def up16(x):
    return -(-x // 16) * 16


def one_hot(hit):
    return jnp.where(hit, 1.0, 0.0).astype(jnp.bfloat16)


def dot(a, b, ca=1, cb=0):
    return lax.dot_general(
        a, b, (((ca,), (cb,)), ((), ())), preferred_element_type=jnp.float32
    )


def pack_kernel(n, hc, width, window, room,
                q_ref, k_ref, v_ref, g_ref, pos_ref, tgt_ref, cnt_ref, out_ref, win):
    tokens = q_ref.shape[0]
    slot = lax.broadcasted_iota(jnp.int32, (n * window, tokens), 0)
    for h in range(hc):
        cols = slice(h * width, (h + 1) * width)
        rows = jnp.concatenate(
            [q_ref[:, cols], k_ref[:, cols], v_ref[:, cols], g_ref[:, cols]], axis=1
        )
        got = dot(one_hot(slot == pos_ref[h]), rows).astype(jnp.bfloat16)
        win[:, h * window:(h + 1) * window, :] = got.reshape(n, window, 4 * width)
    place = lax.broadcasted_iota(jnp.int32, (room, hc * window), 0)
    last = lax.broadcasted_iota(jnp.int32, (room, 4 * width), 0) == room - 1

    def to_owner(o, carry):
        rows = dot(one_hot(place == tgt_ref[o]), win[o])
        out_ref[o] = jnp.where(last, cnt_ref[o], rows).astype(jnp.bfloat16)
        return carry

    lax.fori_loop(0, n, to_owner, 0)


def work_kernel(n, blocks, width, room,
                recv_ref, col_ref, row_ref, valid_ref, out_ref, x, r):
    slots = blocks * SLOT
    scale = width ** (-0.5)
    lane = lax.broadcasted_iota(jnp.int32, (slots, room), 1)
    sublane = lax.broadcasted_iota(jnp.int32, (room, slots), 0)

    def take(s, carry):
        got = dot(one_hot(lane == col_ref[s]), recv_ref[s]).astype(jnp.bfloat16)
        at = pl.ds(pl.multiple_of(s * SLOT, SLOT), SLOT)
        x[:, at, :] = got.reshape(blocks, SLOT, 4 * width)
        return carry

    lax.fori_loop(0, n, take, 0)

    def one(i):
        q = x[i, :, :width]
        k = x[i, :, width:2 * width]
        v = x[i, :, 2 * width:3 * width]
        g = x[i, :, 3 * width:]
        scores = dot(q, k, 1, 1) * scale
        scores = jnp.where(valid_ref[i] > 0, scores, masked_score)
        e = jnp.exp(scores - jnp.max(scores, axis=-1, keepdims=True))
        p = e / jnp.sum(e, axis=-1, keepdims=True)
        w = p.astype(jnp.bfloat16)
        dp = dot(g, v, 1, 1)
        delta = jnp.sum(p * dp, axis=-1, keepdims=True)
        ds = (scale * p * (dp - delta)).astype(jnp.bfloat16)
        r[i, :, :width] = dot(w, v).astype(jnp.bfloat16)
        r[i, :, width:2 * width] = dot(ds, k).astype(jnp.bfloat16)
        r[i, :, 2 * width:3 * width] = dot(ds, q, 0, 0).astype(jnp.bfloat16)
        r[i, :, 3 * width:] = dot(w, g, 0, 0).astype(jnp.bfloat16)

    step = 4 if blocks % 4 == 0 and n * SLOT <= 256 else 1

    def attend(i, carry):
        for j in range(step):
            one(i * step + j)
        return carry

    lax.fori_loop(0, blocks // step, attend, 0)

    def give(s, carry):
        at = pl.ds(pl.multiple_of(s * SLOT, SLOT), SLOT)
        rows = r[:, at, :].reshape(slots, 4 * width)
        out_ref[s] = dot(one_hot(sublane == row_ref[s]), rows).astype(jnp.bfloat16)
        return carry

    lax.fori_loop(0, n, give, 0)


def unpack_kernel(n, hc, width, window, room, earlier, back_ref, pos_ref, tgt_ref, *refs):
    outs, win = refs[earlier:earlier + 4], refs[-1]
    tokens = outs[0].shape[0]
    lane = lax.broadcasted_iota(jnp.int32, (hc * window, room), 1)

    def from_owner(o, carry):
        win[o] = dot(one_hot(lane == tgt_ref[o]), back_ref[o]).astype(jnp.bfloat16)
        return carry

    lax.fori_loop(0, n, from_owner, 0)
    slot = lax.broadcasted_iota(jnp.int32, (tokens, n * window), 1)
    for h in range(hc):
        rows = win[:, h * window:(h + 1) * window, :].reshape(n * window, 4 * width)
        got = dot(one_hot(slot == pos_ref[h]), rows).astype(jnp.bfloat16)
        for f in range(4):
            outs[f][:, h * width:(h + 1) * width] = got[:, f * width:(f + 1) * width]


def full(shape):
    return pl.BlockSpec(shape, lambda i: (0,) * len(shape))


def shards(n, queries, keys, values, grad_out, cluster_ids):
    tok_rows = queries.shape[0]
    heads = cluster_ids.shape[0]
    width = queries.shape[1] // heads
    k = CLUSTERS // n
    chunks = 2 if heads % 2 == 0 else 1
    hc = heads // chunks
    window = up16(k * CAP)
    room = up16(hc * k * CAP * 5 // 6)
    blocks = hc * k
    four = 4 * width
    params = pltpu.CompilerParams(vmem_limit_bytes=VMEM)

    cl = cluster_ids[:, :, 0]
    head_no = jnp.arange(heads, dtype=jnp.int32)[:, None]
    minor = cl // n
    owner = (cl % n + head_no * minor) % n
    cid = owner * k + minor
    names = jnp.arange(CLUSTERS, dtype=jnp.int32)
    member = (cid[:, :, None] == names).astype(jnp.bfloat16)
    tok = jnp.arange(tok_rows)
    earlier = (tok[:, None] > tok[None, :]).astype(jnp.bfloat16)
    before = jnp.einsum("ts,hsc->htc", earlier, member, preferred_element_type=jnp.float32)
    counts = jnp.sum(member.astype(jnp.float32), axis=1)
    same = (names[:, None] // k == names[None, :] // k) & (names[:, None] < names[None, :])
    start = jnp.sum(counts[:, :, None] * same.astype(jnp.float32), axis=1)
    start = start + (names // k * window).astype(jnp.float32)
    pos = jnp.sum(member.astype(jnp.float32) * (before + start[:, None, :]), axis=2)
    pos = pos.astype(jnp.int32)
    seg = jnp.sum(counts.reshape(chunks, hc, n, k), axis=3).astype(jnp.int32)
    ends = jnp.cumsum(seg, axis=1)
    base = ends - seg
    overflow = jnp.max(ends).astype(jnp.int32) > room - 1
    any_overflow = lax.psum(overflow.astype(jnp.float32), tuple(ALL)) > 0
    j = jnp.arange(window, dtype=jnp.int32)
    tgt = jnp.where(j < seg[..., None], base[..., None] + j, -1)
    tgt = jnp.swapaxes(tgt, 1, 2).reshape(chunks, n, hc * window)
    cnt_row = jnp.swapaxes(counts.reshape(chunks, hc, n, k), 1, 2).reshape(chunks, n, 1, blocks)
    cnt_row = jnp.pad(cnt_row, ((0, 0), (0, 0), (0, 0), (0, four - blocks)))

    def pack(c):
        cols = pl.BlockSpec((tok_rows, hc * width), lambda i: (0, c))
        return pl.pallas_call(
            functools.partial(pack_kernel, n, hc, width, window, room),
            grid=(1,),
            out_shape=jax.ShapeDtypeStruct((n, room, four), jnp.bfloat16),
            in_specs=[cols] * 4 + [full((hc, 1, tok_rows)), full((n, 1, hc * window)), full((n, 1, four))],
            out_specs=full((n, room, four)),
            scratch_shapes=[pltpu.VMEM((n, hc * window, four), jnp.bfloat16)],
            compiler_params=params,
            cost_estimate=pl.CostEstimate(flops=6 * 10**9, bytes_accessed=5 * 10**6, transcendentals=0),
        )(queries, keys, values, grad_out,
          pos[c * hc:(c + 1) * hc, None, :], tgt[c][:, None, :], cnt_row[c])

    def work(recv):
        cnt = recv[:, room - 1, :blocks].astype(jnp.float32).astype(jnp.int32)
        lower = jnp.arange(blocks)
        first = jnp.sum(
            jnp.where(lower[:, None] < lower[None, :], cnt[:, :, None], 0), axis=1
        )
        rank = jnp.arange(SLOT, dtype=jnp.int32)
        filled = rank < cnt[..., None]
        source = jnp.where(filled, first[..., None] + rank, -1).reshape(n, blocks * SLOT)
        valid = jnp.swapaxes(filled, 0, 1).reshape(blocks, 1, n * SLOT).astype(jnp.float32)
        return pl.pallas_call(
            functools.partial(work_kernel, n, blocks, width, room),
            out_shape=jax.ShapeDtypeStruct((n, room, four), jnp.bfloat16),
            scratch_shapes=[pltpu.VMEM((blocks, n * SLOT, four), jnp.bfloat16)] * 2,
            compiler_params=params,
            cost_estimate=pl.CostEstimate(flops=10**10, bytes_accessed=5 * 10**6, transcendentals=10**6),
        )(recv, source[:, :, None], source[:, None, :], valid)

    def unpack(c, back, so_far):
        wide = jax.ShapeDtypeStruct((tok_rows, heads * width), jnp.bfloat16)
        cols = pl.BlockSpec((tok_rows, hc * width), lambda i: (0, c))
        return pl.pallas_call(
            functools.partial(unpack_kernel, n, hc, width, window, room, len(so_far)),
            grid=(1,),
            out_shape=[wide] * 4,
            in_specs=[full((n, room, four)), full((hc, tok_rows, 1)), full((n, hc * window, 1))]
            + [pl.BlockSpec(memory_space=pl.ANY)] * len(so_far),
            out_specs=[cols] * 4,
            scratch_shapes=[pltpu.VMEM((n, hc * window, four), jnp.bfloat16)],
            input_output_aliases={3 + i: i for i in range(len(so_far))},
            compiler_params=params,
            cost_estimate=pl.CostEstimate(flops=6 * 10**9, bytes_accessed=5 * 10**6, transcendentals=0),
        )(back, pos[c * hc:(c + 1) * hc, :, None], tgt[c][:, :, None], *so_far)

    def exchange(rows):
        return lax.all_to_all(rows, AXES, split_axis=0, concat_axis=0, tiled=True)

    sent = [exchange(pack(c)) for c in range(chunks)]
    normed = unit_rows(keys.reshape(tok_rows, heads, width).astype(jnp.float32))
    own = (cl[:, :, None] == names).astype(jnp.float32)
    partial_sums = jnp.einsum("htc,thd->hcd", own, normed, precision=lax.Precision.HIGHEST)
    centroid_sums = lax.psum(partial_sums, AXES)
    back = [exchange(work(recv)) for recv in sent]
    outs = ()
    for c in range(chunks - 1):
        outs = unpack(c, back[c], tuple(outs))
    outs = lax.cond(
        any_overflow,
        lambda: padded_path(queries, keys, values, grad_out, cluster_ids),
        lambda: tuple(unpack(chunks - 1, back[-1], tuple(outs))),
    )
    return (*outs, centroid_sums)


ALL = ("groups", "seq", "head", "sub")


def solution(mesh):
    n = mesh.shape["seq"] * mesh.shape["sub"]
    rows = P(("groups", "seq", "sub"), "head")
    return jax.shard_map(
        functools.partial(shards, n),
        mesh=mesh,
        in_specs=(rows, rows, rows, rows, P("head", ("groups", "seq", "sub"), None)),
        out_specs=(rows, rows, rows, rows, P("head", "groups", None)),
        check_vma=False,
    )
```

profile of v0, /device:TPU:0, one launch (start us, length us, event | category | flops | bytes accessed | tf_op | source)
XLA Modules:
  0.0 386.3 jit_solution(4638335844939846575)
XLA Ops:
  9.5 3.1 fusion.56
  16.2 7.2 %shard_map.94 = bf16[8,320,512]{2,1,0:T(8,128)(2,1)} custom-call(bf16[512,1024]{1,0:T(8,128)(2,1)S(1)} %copy-done.1, bf16[512,1024]{1,0:T(8,128)(2,1)S(1)} %copy-done, bf16[512,1024]{1,0:T(8,128)(2,1)} %v_ref.3, bf16[512,1024]{1,0:T(8,128)(2,1)} %g_ref.3, s32[4,1,512]{2,1,0:T(1,128)} %broadcast_in_dim.61.pos_ref, ...), custom_call_target="tpu_custom_call" | custom-call | flops 6000000000 | bytes 5000000 | tf_op jit(solution)/shard_map/pallas_call | solution.py:259
  23.4 6.5 %all-to-all-start.5 = ((bf16[8,320,512]{2,1,0:T(8,128)(2,1)}), bf16[8,320,512]{2,1,0:T(8,128)(2,1)}, u32[]{:S(2)}, u32[]{:S(2)}) async-start(bf16[8,320,512]{2,1,0:T(8,128)(2,1)} %shard_map.94), calls=%async_computation.5 | async-start | bytes 5242880 | tf_op jit(solution)/shard_map/all_to_all | solution.py:306
  31.2 7.1 %shard_map.92 = bf16[8,320,512]{2,1,0:T(8,128)(2,1)} custom-call(bf16[512,1024]{1,0:T(8,128)(2,1)S(1)} %copy-done.1, bf16[512,1024]{1,0:T(8,128)(2,1)S(1)} %copy-done, bf16[512,1024]{1,0:T(8,128)(2,1)S(1)} %copy-done.2, bf16[512,1024]{1,0:T(8,128)(2,1)} %g_ref.3, s32[4,1,512]{2,1,0:T(1,128)} %copy.328.pos_ref, s32[8,1,384]{2,1,0:T(1,128)} %broadcast_in_dim_squeeze.9.tgt_ref, ...), custom_call_target="tpu_custom_call" | custom-call | flops 6000000000 | bytes 5000000 | tf_op jit(solution)/shard_map/pallas_call | solution.py:259
  38.3 52.0 %all-to-all-done.5.recv_ref = bf16[8,320,512]{2,1,0:T(8,128)(2,1)} async-done(((bf16[8,320,512]{2,1,0:T(8,128)(2,1)}), bf16[8,320,512]{2,1,0:T(8,128)(2,1)}, u32[]{:S(2)}, u32[]{:S(2)}) %all-to-all-start.5) | async-done | bytes 2621472 | tf_op jit(solution)/shard_map/all_to_all | solution.py:306
  90.3 4.6 %all-to-all-start.3 = ((bf16[8,320,512]{2,1,0:T(8,128)(2,1)}), bf16[8,320,512]{2,1,0:T(8,128)(2,1)}, u32[]{:S(2)}, u32[]{:S(2)}) async-start(bf16[8,320,512]{2,1,0:T(8,128)(2,1)} %shard_map.92), calls=%async_computation.3 | async-start | bytes 5242880 | tf_op jit(solution)/shard_map/all_to_all | solution.py:306
  95.8 59.2 %all-to-all-done.3.recv_ref = bf16[8,320,512]{2,1,0:T(8,128)(2,1)} async-done(((bf16[8,320,512]{2,1,0:T(8,128)(2,1)}), bf16[8,320,512]{2,1,0:T(8,128)(2,1)}, u32[]{:S(2)}, u32[]{:S(2)}) %all-to-all-start.3) | async-done | bytes 2621472 | tf_op jit(solution)/shard_map/all_to_all | solution.py:306
  157.4 2.5 add.202
  160.1 2.4 lt.301
  162.8 2.5 lt.299
  166.8 5.5 %add_select_fusion.3 = (s32[8,512,1]{2,1,0:T(8,128)}, s32[8,512,1]{2,1,0:T(8,128)}) fusion(s32[8,512,1]{2,1,0:T(8,128)} %add.202, s32[8,512,1]{2,1,0:T(8,128)} %lt.301, s32[512]{0:T(512)S(1)} %lt.272, s32[8,512,1]{2,1,0:T(8,128)S(1)} %add.200, s32[8,512,1]{2,1,0:T(8,128)} %lt.299), kind=kLoop, calls=%fused_computation.86 | loop fusion | flops 24576 | bytes 100352 | tf_op jit(solution)/shard_map/jit(_where)/select_n | solution.py:279
  172.3 26.4 %shard_map.95 = bf16[8,320,512]{2,1,0:T(8,128)(2,1)} custom-call(bf16[8,320,512]{2,1,0:T(8,128)(2,1)} %all-to-all-done.5.recv_ref, s32[8,512,1]{2,1,0:T(8,128)} %get-tuple-element.235.col_ref, s32[8,1,512]{2,1,0:T(1,128)} %get-tuple-element.233.row_ref, f32[32,1,128]{2,1,0:T(1,128)} %get-tuple-element.227.valid_ref), custom_call_target="tpu_custom_call" | custom-call | flops 10000000000 | bytes 5000000 | tf_op jit(solution)/shard_map/pallas_call | solution.py:281
  198.7 4.4 %all-to-all-start.6 = ((bf16[8,320,512]{2,1,0:T(8,128)(2,1)}), bf16[8,320,512]{2,1,0:T(8,128)(2,1)}, u32[]{:S(2)}, u32[]{:S(2)}) async-start(bf16[8,320,512]{2,1,0:T(8,128)(2,1)} %shard_map.95), calls=%async_computation.6 | async-start | bytes 5242880 | tf_op jit(solution)/shard_map/all_to_all | solution.py:306
  203.1 26.4 %shard_map.93 = bf16[8,320,512]{2,1,0:T(8,128)(2,1)} custom-call(bf16[8,320,512]{2,1,0:T(8,128)(2,1)} %all-to-all-done.3.recv_ref, s32[8,512,1]{2,1,0:T(8,128)} %get-tuple-element.236.col_ref, s32[8,1,512]{2,1,0:T(1,128)} %get-tuple-element.234.row_ref, f32[32,1,128]{2,1,0:T(1,128)} %get-tuple-element.228.valid_ref), custom_call_target="tpu_custom_call" | custom-call | flops 10000000000 | bytes 5000000 | tf_op jit(solution)/shard_map/pallas_call | solution.py:281
  229.5 33.9 %all-to-all-done.6.back_ref = bf16[8,320,512]{2,1,0:T(8,128)(2,1)} async-done(((bf16[8,320,512]{2,1,0:T(8,128)(2,1)}), bf16[8,320,512]{2,1,0:T(8,128)(2,1)}, u32[]{:S(2)}, u32[]{:S(2)}) %all-to-all-start.6) | async-done | bytes 2621472 | tf_op jit(solution)/shard_map/all_to_all | solution.py:306
  263.4 4.4 %all-to-all-start.4 = ((bf16[8,320,512]{2,1,0:T(8,128)(2,1)}), bf16[8,320,512]{2,1,0:T(8,128)(2,1)}, u32[]{:S(2)}, u32[]{:S(2)}) async-start(bf16[8,320,512]{2,1,0:T(8,128)(2,1)} %shard_map.93), calls=%async_computation.4 | async-start | bytes 5242880 | tf_op jit(solution)/shard_map/all_to_all | solution.py:306
  271.2 1.8 fusion.57
  273.0 78.6 %psum.14 = f32[]{:T(128)} all-reduce(f32[]{:T(128)S(6)} %convert_element_type.171), channel_id=1, replica_groups=mesh['groups'=2,'seq'=4,'head'=2,'sub'=2] {'groups','seq','head','sub'}, use_global_device_ids=true, to_apply=%region_4.5 | all-reduce | flops 1 | bytes 8 | tf_op jit(solution)/shard_map/psum | solution.py:250
  351.6 2.6 broadcast_in_dim_squeeze.12.tgt_ref
  356.2 9.0 %shard_map.96 = (bf16[512,1024]{1,0:T(8,128)(2,1)}, bf16[512,1024]{1,0:T(8,128)(2,1)}, bf16[512,1024]{1,0:T(8,128)(2,1)}, bf16[512,1024]{1,0:T(8,128)(2,1)}) custom-call(bf16[8,320,512]{2,1,0:T(8,128)(2,1)} %all-to-all-done.6.back_ref, s32[4,512,1]{2,1,0:T(8,128)} %copy.341.pos_ref, s32[8,384,1]{2,1,0:T(8,128)} %broadcast_in_dim_squeeze.12.tgt_ref), custom_call_target="tpu_custom_call" | custom-call | flops 6000000000 | bytes 5000000 | tf_op jit(solution)/shard_map/pallas_call | solution.py:292
  365.3 12.5 %conditional.1 = ((bf16[512,1024]{1,0:T(8,128)(2,1)}, bf16[512,1024]{1,0:T(8,128)(2,1)}, bf16[512,1024]{1,0:T(8,128)(2,1)}, bf16[512,1024]{1,0:T(8,128)(2,1)})) conditional(s32[]{:T(128)} %convert_element_type.172, (s32[8,512]{1,0:T(8,128)S(1)}, s32[4,96]{1,0:T(4,128)S(1)}, s32[4,96]{1,0:T(4,128)S(1)}, s32[2,8,4,96]{3,2,1,0:T(4,128)S(1)}, ...), branch_computations={%region_9.10_spmd, %region_10.18_spmd} | conditional | flops 7451324416 | bytes 243533728 | solution.py:317
  365.8 1.7 copy.289.tgt_ref
  368.9 9.0 %branch_0_fun.1 = (bf16[512,1024]{1,0:T(8,128)(2,1)}, bf16[512,1024]{1,0:T(8,128)(2,1)}, bf16[512,1024]{1,0:T(8,128)(2,1)}, bf16[512,1024]{1,0:T(8,128)(2,1)}) custom-call(bf16[8,320,512]{2,1,0:T(8,128)(2,1)} %get-tuple-element.40.back_ref, s32[4,512,1]{2,1,0:T(8,128)} %copy.288.pos_ref, ...), custom_call_target="tpu_custom_call", output_to_operand_aliasing={{0}: (3, {}), {1}: (4, {}), {2}: (5, {}), {3}: (6, {})} | custom-call | flops 6000000000 | bytes 5000000 | tf_op jit(solution)/shard_map/cond/branch_0_fun/pallas_call | solution.py:292
  377.8 1.7 copy.424
  (83 shorter events, 18.2 us)
Async XLA Ops:
  7.2 1.4 copy-start.5
  12.6 3.6 copy-start
  12.6 3.6 copy-start.1
  23.4 7.8 %copy-start.2 = (bf16[512,1024]{1,0:T(8,128)(2,1)S(1)}, bf16[512,1024]{1,0:T(8,128)(2,1)}, u32[]{:S(2)}) copy-start(bf16[512,1024]{1,0:T(8,128)(2,1)} %v_ref.3) | copy-start | bytes 3145732
  23.4 66.9 %all-to-all-start.5 = ((bf16[8,320,512]{2,1,0:T(8,128)(2,1)}), bf16[8,320,512]{2,1,0:T(8,128)(2,1)}, u32[]{:S(2)}, u32[]{:S(2)}) async-start(bf16[8,320,512]{2,1,0:T(8,128)(2,1)} %shard_map.94), calls=%async_computation.5 | async-start | bytes 5242880 | tf_op jit(solution)/shard_map/all_to_all | solution.py:306
  90.3 64.7 %all-to-all-start.3 = ((bf16[8,320,512]{2,1,0:T(8,128)(2,1)}), bf16[8,320,512]{2,1,0:T(8,128)(2,1)}, u32[]{:S(2)}, u32[]{:S(2)}) async-start(bf16[8,320,512]{2,1,0:T(8,128)(2,1)} %shard_map.92), calls=%async_computation.3 | async-start | bytes 5242880 | tf_op jit(solution)/shard_map/all_to_all | solution.py:306
  198.7 64.7 %all-to-all-start.6 = ((bf16[8,320,512]{2,1,0:T(8,128)(2,1)}), bf16[8,320,512]{2,1,0:T(8,128)(2,1)}, u32[]{:S(2)}, u32[]{:S(2)}) async-start(bf16[8,320,512]{2,1,0:T(8,128)(2,1)} %shard_map.95), calls=%async_computation.6 | async-start | bytes 5242880 | tf_op jit(solution)/shard_map/all_to_all | solution.py:306
  263.4 101.8 %all-to-all-start.4 = ((bf16[8,320,512]{2,1,0:T(8,128)(2,1)}), bf16[8,320,512]{2,1,0:T(8,128)(2,1)}, u32[]{:S(2)}, u32[]{:S(2)}) async-start(bf16[8,320,512]{2,1,0:T(8,128)(2,1)} %shard_map.93), calls=%async_computation.4 | async-start | bytes 5242880 | tf_op jit(solution)/shard_map/all_to_all | solution.py:306
  267.8 110.0 %all-reduce.3.cloned.1.call-start = ((), (), s32[]{:S(2)}) async-start(), calls=%async_computation.7 | async-start | bytes 524288 | tf_op jit(solution)/shard_map/psum | solution.py:312
Sparse Core Ops, SparseCore 0:
  273.2 72.9 all-reduce.2
where the time goes:
time: 387 us; the launch traced here: 386 us
  waiting for transfers between devices  145 us (37%)
  Pallas kernels  85.1 us (22%)
  blocking collectives  78.6 us (20%)
  local copies, waits for them, and re-layouts  25.3 us (7%)
  starting transfers between devices  19.9 us (5%)
  between operations  15.7 us (4%)
  other arithmetic  14.4 us (4%)
    all_to_all x4, waiting for transfers between devices, exchange(): return lax.all_to_all(rows, AXES, split_axis=0, concat_axis=0, tiled=True)  145 us
    psum x1, blocking collectives, shards(): any_overflow = lax.psum(overflow.astype(jnp.float32), tuple(ALL)) > 0  78.6 us
    pallas_call x2, Pallas kernels, work(): pl.pallas_call(functools.partial(work_kernel, n, blocks, width, room), ou...  52.8 us
    all_to_all x4, starting transfers between devices, exchange(): return lax.all_to_all(rows, AXES, split_axis=0, concat_axis=0, tiled=True)  19.8 us
    pallas_call x2, Pallas kernels, unpack(): pl.pallas_call(functools.partial(unpack_kernel, n, hc, width, window, roo...  17.9 us
    pallas_call x2, Pallas kernels, pack(): pl.pallas_call(functools.partial(pack_kernel, n, hc, width, window, room)...  14.3 us
  transfers between devices with their start and end apart: 5, of which 3 were waited for; matrix products, arithmetic and copies ran while one was open for 4% of the time, Pallas kernels for 13%

commit v1 on v0

--- a/solution.py
+++ b/solution.py
@@ -141,15 +141,29 @@
     lax.fori_loop(0, n, to_owner, 0)
 
 
-def work_kernel(n, blocks, width, room,
-                recv_ref, col_ref, row_ref, valid_ref, out_ref, x, r):
+def work_kernel(n, blocks, width, room, recv_ref, out_ref, x, r, from_row, filled):
     slots = blocks * SLOT
     scale = width ** (-0.5)
-    lane = lax.broadcasted_iota(jnp.int32, (slots, room), 1)
     sublane = lax.broadcasted_iota(jnp.int32, (room, slots), 0)
+    iota = functools.partial(lax.broadcasted_iota, jnp.int32)
+
+    tails = recv_ref[:, room - 16:, :128].reshape(n * 16, 128)
+    lane, block = iota((128, slots), 0), iota((128, slots), 1) // SLOT
+    count = dot(tails, one_hot(lane == block))
+    first = dot(tails, one_hot(lane < block))
+    rank = (iota((n * 16, slots), 1) % SLOT).astype(jnp.float32)
+    from_row[...] = jnp.where(rank < count, first + rank, -1.0).reshape(n, 16, slots)
+    shape = (n * 16, n * SLOT)
+    tail_of = one_hot(iota(shape, 0) == iota(shape, 1) // SLOT * 16 + 15)
+    per_block = dot(tails, tail_of, 0, 0)
+    rank = (iota((128, n * SLOT), 1) % SLOT).astype(jnp.float32)
+    filled[...] = jnp.where(rank < per_block, 1.0, 0.0)
+
+    def places(s):
+        return one_hot(sublane == from_row[s, 15:16, :].astype(jnp.int32))
 
     def take(s, carry):
-        got = dot(one_hot(lane == col_ref[s]), recv_ref[s]).astype(jnp.bfloat16)
+        got = dot(places(s), recv_ref[s], 0, 0).astype(jnp.bfloat16)
         at = pl.ds(pl.multiple_of(s * SLOT, SLOT), SLOT)
         x[:, at, :] = got.reshape(blocks, SLOT, 4 * width)
         return carry
@@ -162,7 +176,7 @@
         v = x[i, :, 2 * width:3 * width]
         g = x[i, :, 3 * width:]
         scores = dot(q, k, 1, 1) * scale
-        scores = jnp.where(valid_ref[i] > 0, scores, masked_score)
+        scores = jnp.where(filled[pl.ds(i, 1), :] > 0, scores, masked_score)
         e = jnp.exp(scores - jnp.max(scores, axis=-1, keepdims=True))
         p = e / jnp.sum(e, axis=-1, keepdims=True)
         w = p.astype(jnp.bfloat16)
@@ -186,7 +200,7 @@
     def give(s, carry):
         at = pl.ds(pl.multiple_of(s * SLOT, SLOT), SLOT)
         rows = r[:, at, :].reshape(slots, 4 * width)
-        out_ref[s] = dot(one_hot(sublane == row_ref[s]), rows).astype(jnp.bfloat16)
+        out_ref[s] = dot(places(s), rows).astype(jnp.bfloat16)
         return carry
 
     lax.fori_loop(0, n, give, 0)
@@ -195,17 +209,17 @@
 def unpack_kernel(n, hc, width, window, room, earlier, back_ref, pos_ref, tgt_ref, *refs):
     outs, win = refs[earlier:earlier + 4], refs[-1]
     tokens = outs[0].shape[0]
-    lane = lax.broadcasted_iota(jnp.int32, (hc * window, room), 1)
+    place = lax.broadcasted_iota(jnp.int32, (room, hc * window), 0)
 
     def from_owner(o, carry):
-        win[o] = dot(one_hot(lane == tgt_ref[o]), back_ref[o]).astype(jnp.bfloat16)
+        win[o] = dot(one_hot(place == tgt_ref[o]), back_ref[o], 0, 0).astype(jnp.bfloat16)
         return carry
 
     lax.fori_loop(0, n, from_owner, 0)
-    slot = lax.broadcasted_iota(jnp.int32, (tokens, n * window), 1)
+    slot = lax.broadcasted_iota(jnp.int32, (n * window, tokens), 0)
     for h in range(hc):
         rows = win[:, h * window:(h + 1) * window, :].reshape(n * window, 4 * width)
-        got = dot(one_hot(slot == pos_ref[h]), rows).astype(jnp.bfloat16)
+        got = dot(one_hot(slot == pos_ref[h]), rows, 0, 0).astype(jnp.bfloat16)
         for f in range(4):
             outs[f][:, h * width:(h + 1) * width] = got[:, f * width:(f + 1) * width]
 
@@ -246,13 +260,14 @@
     seg = jnp.sum(counts.reshape(chunks, hc, n, k), axis=3).astype(jnp.int32)
     ends = jnp.cumsum(seg, axis=1)
     base = ends - seg
-    overflow = jnp.max(ends).astype(jnp.int32) > room - 1
-    any_overflow = lax.psum(overflow.astype(jnp.float32), tuple(ALL)) > 0
+    overflow = (jnp.max(ends) > room - 1).astype(jnp.float32)
     j = jnp.arange(window, dtype=jnp.int32)
     tgt = jnp.where(j < seg[..., None], base[..., None] + j, -1)
     tgt = jnp.swapaxes(tgt, 1, 2).reshape(chunks, n, hc * window)
     cnt_row = jnp.swapaxes(counts.reshape(chunks, hc, n, k), 1, 2).reshape(chunks, n, 1, blocks)
-    cnt_row = jnp.pad(cnt_row, ((0, 0), (0, 0), (0, 0), (0, four - blocks)))
+    flag = jnp.broadcast_to(overflow, (chunks, n, 1, 1))
+    rest = jnp.zeros((chunks, n, 1, four - blocks - 1), jnp.float32)
+    cnt_row = jnp.concatenate([cnt_row, flag, rest], axis=3)
 
     def pack(c):
         cols = pl.BlockSpec((tok_rows, hc * width), lambda i: (0, c))
@@ -269,22 +284,17 @@
           pos[c * hc:(c + 1) * hc, None, :], tgt[c][:, None, :], cnt_row[c])
 
     def work(recv):
-        cnt = recv[:, room - 1, :blocks].astype(jnp.float32).astype(jnp.int32)
-        lower = jnp.arange(blocks)
-        first = jnp.sum(
-            jnp.where(lower[:, None] < lower[None, :], cnt[:, :, None], 0), axis=1
-        )
-        rank = jnp.arange(SLOT, dtype=jnp.int32)
-        filled = rank < cnt[..., None]
-        source = jnp.where(filled, first[..., None] + rank, -1).reshape(n, blocks * SLOT)
-        valid = jnp.swapaxes(filled, 0, 1).reshape(blocks, 1, n * SLOT).astype(jnp.float32)
         return pl.pallas_call(
             functools.partial(work_kernel, n, blocks, width, room),
             out_shape=jax.ShapeDtypeStruct((n, room, four), jnp.bfloat16),
-            scratch_shapes=[pltpu.VMEM((blocks, n * SLOT, four), jnp.bfloat16)] * 2,
+            scratch_shapes=[pltpu.VMEM((blocks, n * SLOT, four), jnp.bfloat16)] * 2
+            + [
+                pltpu.VMEM((n, 16, blocks * SLOT), jnp.float32),
+                pltpu.VMEM((128, n * SLOT), jnp.float32),
+            ],
             compiler_params=params,
             cost_estimate=pl.CostEstimate(flops=10**10, bytes_accessed=5 * 10**6, transcendentals=10**6),
-        )(recv, source[:, :, None], source[:, None, :], valid)
+        )(recv)
 
     def unpack(c, back, so_far):
         wide = jax.ShapeDtypeStruct((tok_rows, heads * width), jnp.bfloat16)
@@ -293,14 +303,14 @@
             functools.partial(unpack_kernel, n, hc, width, window, room, len(so_far)),
             grid=(1,),
             out_shape=[wide] * 4,
-            in_specs=[full((n, room, four)), full((hc, tok_rows, 1)), full((n, hc * window, 1))]
+            in_specs=[full((n, room, four)), full((hc, 1, tok_rows)), full((n, 1, hc * window))]
             + [pl.BlockSpec(memory_space=pl.ANY)] * len(so_far),
             out_specs=[cols] * 4,
             scratch_shapes=[pltpu.VMEM((n, hc * window, four), jnp.bfloat16)],
             input_output_aliases={3 + i: i for i in range(len(so_far))},
             compiler_params=params,
             cost_estimate=pl.CostEstimate(flops=6 * 10**9, bytes_accessed=5 * 10**6, transcendentals=0),
-        )(back, pos[c * hc:(c + 1) * hc, :, None], tgt[c][:, :, None], *so_far)
+        )(back, pos[c * hc:(c + 1) * hc, None, :], tgt[c][:, None, :], *so_far)
 
     def exchange(rows):
         return lax.all_to_all(rows, AXES, split_axis=0, concat_axis=0, tiled=True)
@@ -315,14 +325,11 @@
     for c in range(chunks - 1):
         outs = unpack(c, back[c], tuple(outs))
     outs = lax.cond(
-        any_overflow,
+        jnp.max(sent[0][:, room - 1, blocks]) > 0,
         lambda: padded_path(queries, keys, values, grad_out, cluster_ids),
         lambda: tuple(unpack(chunks - 1, back[-1], tuple(outs))),
     )
     return (*outs, centroid_sums)
-
-
-ALL = ("groups", "seq", "head", "sub")
 
 
 def solution(mesh):

time: 387 us -> 306 us (0.79)
  blocking collectives: 78.6 us -> 0 us
  waiting for transfers between devices: 145 us -> 172 us
  local copies, waits for them, and re-layouts: 25.3 us -> 7.13 us
  other arithmetic: 14.4 us -> 5.75 us
    psum x1 -> x0, blocking collectives: 78.6 us -> none  [shards(): any_overflow = lax.psum(overflow.astype(jnp.float32), tuple(ALL)) > 0]
    all_to_all x4, waiting for transfers between devices: 145 us -> 172 us  [exchange(): return lax.all_to_all(rows, AXES, split_axis=0, concat_axis=0, tiled=True)]
    select_n x2 -> x0, other arithmetic: 6.15 us -> none  [work(): jnp.where(filled, first[..., None] + rank, -1).reshape(n, blocks * SLOT)]
    lt x15 -> x0, local copies, waits for them, and re-layouts: 5.64 us -> none  [work(): filled = rank < cnt[..., None]]
    add x6 -> x0, local copies, waits for them, and re-layouts: 4.04 us -> none  [work(): first[..., None] + rank]
  transfers between devices with their start and end apart: 5 -> 5, of which waited for: 3 -> 4; matrix products, arithmetic and copies ran while one was open for 4% -> 3% of each run, Pallas kernels for 13% -> 25%
where the time goes in v1:
time: 306 us; the launch traced here: 305 us
  waiting for transfers between devices  172 us (56%)
  Pallas kernels  82.4 us (27%)
  starting transfers between devices  20 us (7%)
  between operations  15.5 us (5%)
  local copies, waits for them, and re-layouts  7.13 us (2%)
  other arithmetic  5.75 us (2%)
    all_to_all x4, waiting for transfers between devices, exchange(): return lax.all_to_all(rows, AXES, split_axis=0, concat_axis=0, tiled=True)  172 us
    pallas_call x2, Pallas kernels, work(): pl.pallas_call(functools.partial(work_kernel, n, blocks, width, room), ou...  51.7 us
    all_to_all x4, starting transfers between devices, exchange(): return lax.all_to_all(rows, AXES, split_axis=0, concat_axis=0, tiled=True)  19.8 us
    pallas_call x2, Pallas kernels, unpack(): pl.pallas_call(functools.partial(unpack_kernel, n, hc, width, window, roo...  16 us
    pallas_call x2, Pallas kernels, pack(): pl.pallas_call(functools.partial(pack_kernel, n, hc, width, window, room)...  14.7 us
  transfers between devices with their start and end apart: 5, of which 4 were waited for; matrix products, arithmetic and copies ran while one was open for 3% of the time, Pallas kernels for 25%

profile of v1, /device:TPU:0, one launch (start us, length us, event | category | flops | bytes accessed | tf_op | source)
XLA Modules:
  0.0 305.0 jit_solution(15531051944673936172)
XLA Ops:
  7.2 0.9 fusion.65
  8.8 0.7 broadcast_in_dim_squeeze.7.tgt_ref
  9.5 0.6 reduce_max.27
  11.1 0.6 slice_bitcast_fusion
  13.1 7.5 %shard_map.92 = bf16[8,320,512]{2,1,0:T(8,128)(2,1)} custom-call(bf16[512,1024]{1,0:T(8,128)(2,1)} %q_ref.3, bf16[512,1024]{1,0:T(8,128)(2,1)} %k_ref.3, bf16[512,1024]{1,0:T(8,128)(2,1)} %v_ref.3, bf16[512,1024]{1,0:T(8,128)(2,1)} %g_ref.3, s32[4,1,512]{2,1,0:T(1,128)} %broadcast_in_dim.26.pos_ref, s32[8,1,384]{2,1,0:T(1,128)} %broadcast_in_dim_squeeze.7.tgt_ref, ...), custom_call_target="tpu_custom_call" | custom-call | flops 6000000000 | bytes 5000000 | tf_op jit(solution)/shard_map/pallas_call | solution.py:274
  20.7 6.6 %all-to-all-start.3 = ((bf16[8,320,512]{2,1,0:T(8,128)(2,1)}), bf16[8,320,512]{2,1,0:T(8,128)(2,1)}, u32[]{:S(2)}, u32[]{:S(2)}) async-start(bf16[8,320,512]{2,1,0:T(8,128)(2,1)} %shard_map.92), calls=%async_computation.3 | async-start | bytes 5242880 | tf_op jit(solution)/shard_map/all_to_all | solution.py:316
  27.3 0.7 broadcast_in_dim_squeeze.8.tgt_ref
  28.6 7.2 %shard_map.93 = bf16[8,320,512]{2,1,0:T(8,128)(2,1)} custom-call(bf16[512,1024]{1,0:T(8,128)(2,1)S(1)} %copy-done.1, bf16[512,1024]{1,0:T(8,128)(2,1)S(1)} %copy-done, bf16[512,1024]{1,0:T(8,128)(2,1)S(1)} %copy-done.3, bf16[512,1024]{1,0:T(8,128)(2,1)} %g_ref.3, s32[4,1,512]{2,1,0:T(1,128)} %copy.225.pos_ref, s32[8,1,384]{2,1,0:T(1,128)} %broadcast_in_dim_squeeze.8.tgt_ref, ...), custom_call_target="tpu_custom_call" | custom-call | flops 6000000000 | bytes 5000000 | tf_op jit(solution)/shard_map/pallas_call | solution.py:274
  35.7 51.9 %all-to-all-done.3.recv_ref = bf16[8,320,512]{2,1,0:T(8,128)(2,1)} async-done(((bf16[8,320,512]{2,1,0:T(8,128)(2,1)}), bf16[8,320,512]{2,1,0:T(8,128)(2,1)}, u32[]{:S(2)}, u32[]{:S(2)}) %all-to-all-start.3) | async-done | bytes 2621472 | tf_op jit(solution)/shard_map/all_to_all | solution.py:316
  87.7 4.4 %all-to-all-start.4 = ((bf16[8,320,512]{2,1,0:T(8,128)(2,1)}), bf16[8,320,512]{2,1,0:T(8,128)(2,1)}, u32[]{:S(2)}, u32[]{:S(2)}) async-start(bf16[8,320,512]{2,1,0:T(8,128)(2,1)} %shard_map.93), calls=%async_computation.4 | async-start | bytes 5242880 | tf_op jit(solution)/shard_map/all_to_all | solution.py:316
  92.1 25.8 %shard_map.95 = bf16[8,320,512]{2,1,0:T(8,128)(2,1)} custom-call(bf16[8,320,512]{2,1,0:T(8,128)(2,1)} %all-to-all-done.3.recv_ref), custom_call_target="tpu_custom_call" | custom-call | flops 10000000000 | bytes 5000000 | tf_op jit(solution)/shard_map/pallas_call | solution.py:287
  117.9 34.5 %all-to-all-done.4.recv_ref = bf16[8,320,512]{2,1,0:T(8,128)(2,1)} async-done(((bf16[8,320,512]{2,1,0:T(8,128)(2,1)}), bf16[8,320,512]{2,1,0:T(8,128)(2,1)}, u32[]{:S(2)}, u32[]{:S(2)}) %all-to-all-start.4) | async-done | bytes 2621472 | tf_op jit(solution)/shard_map/all_to_all | solution.py:316
  152.4 4.4 %all-to-all-start.6 = ((bf16[8,320,512]{2,1,0:T(8,128)(2,1)}), bf16[8,320,512]{2,1,0:T(8,128)(2,1)}, u32[]{:S(2)}, u32[]{:S(2)}) async-start(bf16[8,320,512]{2,1,0:T(8,128)(2,1)} %shard_map.95), calls=%async_computation.6 | async-start | bytes 5242880 | tf_op jit(solution)/shard_map/all_to_all | solution.py:316
  156.8 25.8 %shard_map.94 = bf16[8,320,512]{2,1,0:T(8,128)(2,1)} custom-call(bf16[8,320,512]{2,1,0:T(8,128)(2,1)} %all-to-all-done.4.recv_ref), custom_call_target="tpu_custom_call" | custom-call | flops 10000000000 | bytes 5000000 | tf_op jit(solution)/shard_map/pallas_call | solution.py:287
  182.6 34.5 %all-to-all-done.6.back_ref = bf16[8,320,512]{2,1,0:T(8,128)(2,1)} async-done(((bf16[8,320,512]{2,1,0:T(8,128)(2,1)}), bf16[8,320,512]{2,1,0:T(8,128)(2,1)}, u32[]{:S(2)}, u32[]{:S(2)}) %all-to-all-start.6) | async-done | bytes 2621472 | tf_op jit(solution)/shard_map/all_to_all | solution.py:316
  217.1 4.4 %all-to-all-start.5 = ((bf16[8,320,512]{2,1,0:T(8,128)(2,1)}), bf16[8,320,512]{2,1,0:T(8,128)(2,1)}, u32[]{:S(2)}, u32[]{:S(2)}) async-start(bf16[8,320,512]{2,1,0:T(8,128)(2,1)} %shard_map.94), calls=%async_computation.5 | async-start | bytes 5242880 | tf_op jit(solution)/shard_map/all_to_all | solution.py:316
  223.7 1.8 fusion.51
  225.6 1.4 slice_reduce_fusion
  227.7 8.0 %shard_map.96 = (bf16[512,1024]{1,0:T(8,128)(2,1)}, bf16[512,1024]{1,0:T(8,128)(2,1)}, bf16[512,1024]{1,0:T(8,128)(2,1)}, bf16[512,1024]{1,0:T(8,128)(2,1)}) custom-call(bf16[8,320,512]{2,1,0:T(8,128)(2,1)} %all-to-all-done.6.back_ref, s32[4,1,512]{2,1,0:T(1,128)} %broadcast_in_dim.26.pos_ref, s32[8,1,384]{2,1,0:T(1,128)} %broadcast_in_dim_squeeze.7.tgt_ref), custom_call_target="tpu_custom_call" | custom-call | flops 6000000000 | bytes 5000000 | tf_op jit(solution)/shard_map/pallas_call | solution.py:302
  235.7 50.9 %all-to-all-done.5 = bf16[8,320,512]{2,1,0:T(8,128)(2,1)} async-done(((bf16[8,320,512]{2,1,0:T(8,128)(2,1)}), bf16[8,320,512]{2,1,0:T(8,128)(2,1)}, u32[]{:S(2)}, u32[]{:S(2)}) %all-to-all-start.5) | async-done | bytes 2621472 | tf_op jit(solution)/shard_map/all_to_all | solution.py:316
  286.7 9.8 %conditional.1 = ((bf16[512,1024]{1,0:T(8,128)(2,1)}, bf16[512,1024]{1,0:T(8,128)(2,1)}, bf16[512,1024]{1,0:T(8,128)(2,1)}, bf16[512,1024]{1,0:T(8,128)(2,1)})) conditional(s32[]{:T(128)} %convert_element_type.132, (s32[8,512]{1,0:T(8,128)S(1)}, s32[4,96]{1,0:T(4,128)S(1)}, s32[4,96]{1,0:T(4,128)S(1)}, s32[2,8,4,96]{3,2,0,1:T(4,128)S(1)}, ...), branch_computations={%region_7.8_spmd, %region_8.16_spmd} | conditional | flops 7451324416 | bytes 251922400 | solution.py:327
  287.3 0.6 fusion.tgt_ref
  288.5 8.0 %branch_0_fun.1 = (bf16[512,1024]{1,0:T(8,128)(2,1)}, bf16[512,1024]{1,0:T(8,128)(2,1)}, bf16[512,1024]{1,0:T(8,128)(2,1)}, bf16[512,1024]{1,0:T(8,128)(2,1)}) custom-call(bf16[8,320,512]{2,1,0:T(8,128)(2,1)} %get-tuple-element.40.back_ref, ...), custom_call_target="tpu_custom_call", output_to_operand_aliasing={{0}: (3, {}), {1}: (4, {}), {2}: (5, {}), {3}: (6, {})} | custom-call | flops 6000000000 | bytes 5000000 | tf_op jit(solution)/shard_map/cond/branch_0_fun/pallas_call | solution.py:302
  296.5 1.7 copy.307
  (54 shorter events, 6.4 us)
Async XLA Ops:
  20.7 7.9 %copy-start = (bf16[512,1024]{1,0:T(8,128)(2,1)S(1)}, bf16[512,1024]{1,0:T(8,128)(2,1)}, u32[]{:S(2)}) copy-start(bf16[512,1024]{1,0:T(8,128)(2,1)} %k_ref.3) | copy-start | bytes 3145732
  20.7 7.9 %copy-start.1 = (bf16[512,1024]{1,0:T(8,128)(2,1)S(1)}, bf16[512,1024]{1,0:T(8,128)(2,1)}, u32[]{:S(2)}) copy-start(bf16[512,1024]{1,0:T(8,128)(2,1)} %q_ref.3) | copy-start | bytes 3145732
  20.7 7.9 %copy-start.3 = (bf16[512,1024]{1,0:T(8,128)(2,1)S(1)}, bf16[512,1024]{1,0:T(8,128)(2,1)}, u32[]{:S(2)}) copy-start(bf16[512,1024]{1,0:T(8,128)(2,1)} %v_ref.3) | copy-start | bytes 3145732
  20.7 67.0 %all-to-all-start.3 = ((bf16[8,320,512]{2,1,0:T(8,128)(2,1)}), bf16[8,320,512]{2,1,0:T(8,128)(2,1)}, u32[]{:S(2)}, u32[]{:S(2)}) async-start(bf16[8,320,512]{2,1,0:T(8,128)(2,1)} %shard_map.92), calls=%async_computation.3 | async-start | bytes 5242880 | tf_op jit(solution)/shard_map/all_to_all | solution.py:316
  87.7 64.7 %all-to-all-start.4 = ((bf16[8,320,512]{2,1,0:T(8,128)(2,1)}), bf16[8,320,512]{2,1,0:T(8,128)(2,1)}, u32[]{:S(2)}, u32[]{:S(2)}) async-start(bf16[8,320,512]{2,1,0:T(8,128)(2,1)} %shard_map.93), calls=%async_computation.4 | async-start | bytes 5242880 | tf_op jit(solution)/shard_map/all_to_all | solution.py:316
  152.4 64.7 %all-to-all-start.6 = ((bf16[8,320,512]{2,1,0:T(8,128)(2,1)}), bf16[8,320,512]{2,1,0:T(8,128)(2,1)}, u32[]{:S(2)}, u32[]{:S(2)}) async-start(bf16[8,320,512]{2,1,0:T(8,128)(2,1)} %shard_map.95), calls=%async_computation.6 | async-start | bytes 5242880 | tf_op jit(solution)/shard_map/all_to_all | solution.py:316
  182.6 39.1 %copy-start.7 = (s32[8,512,1]{1,2,0:T(1,128)S(1)}, s32[8,512,1]{1,2,0:T(1,128)}, u32[]{:S(2)}) copy-start(s32[8,512,1]{1,2,0:T(1,128)} %param.11) | copy-start | bytes 49156
  217.1 69.5 %all-to-all-start.5 = ((bf16[8,320,512]{2,1,0:T(8,128)(2,1)}), bf16[8,320,512]{2,1,0:T(8,128)(2,1)}, u32[]{:S(2)}, u32[]{:S(2)}) async-start(bf16[8,320,512]{2,1,0:T(8,128)(2,1)} %shard_map.94), calls=%async_computation.5 | async-start | bytes 5242880 | tf_op jit(solution)/shard_map/all_to_all | solution.py:316
  221.5 75.0 %all-reduce.2.cloned.1.call-start = ((), (), s32[]{:S(2)}) async-start(), calls=%async_computation.7 | async-start | bytes 524288 | tf_op jit(solution)/shard_map/psum | solution.py:322
Sparse Core Ops, SparseCore 0:
  225.7 63.1 all-reduce.1
